TPU v7x, 256 devices: a whole 4x4x8 slice. The times are simulated.
256 devices in a mesh: row: 16 (over y, x_lo, core), col: 16 (over z, x_hi).
Axes of the slice: x: 4 (x_hi: 2, x_lo: 2; x = x_hi * 2 + x_lo), y: 4, z: 8, core: 2. Of those that a mesh axis runs over, the one named last changes fastest.
Arguments:
- inverse_rows: float32 [16384, 16384], P('col', 'row'), may hold values from -0.5 to 0.5
- panels: float32 [16, 16384, 256], P('col', 'row'), may hold values from -0.75 to 0.75
- diag_inverse: float32 [2, 256, 256], replicated, may hold values from -12 to 12
- pattern: int32 [2, 64], replicated, may hold values 0 or 1
- owner_slot: int32 [2], replicated, may hold values from 0 to 15, as said below
Outputs:
- inverse_column: float32 [2, 16384, 256], P(None, 'row')
- inverse_row: float32 [2, 256, 16384], P(None, None, 'col')
- diag_block: float32 [2, 256, 256], replicated
Inputs may be any that keep to these rules, and one draw needn't show every extreme that they name: `owner_slot`: the two supernodes' panels lie in two different slots, one of them the last slot.
All inputs are finite; a program needn't handle non-finite values.
Results may differ from a plain program's by a relative error of at most 0.0001.
Values sent between devices are 32-bit elements; how exact they have to be, the bound alone decides.
No kernel may reach another device: no remote copies, remote signals or barrier semaphores. Data moves between devices by JAX's collectives and lax.ppermute only.
A program may use at most 64 MiB of HBM per device.

v0:
```python
import jax
import jax.numpy as jnp
from jax import lax
from jax.sharding import PartitionSpec as P


def from_root(array, axis, root):
    mine = lax.axis_index(axis) == root
    return lax.psum(jnp.where(mine, array, jnp.zeros_like(array)), axis)


def block_mask(pattern_row, start_block, count_blocks, width):
    live = lax.dynamic_slice_in_dim(pattern_row, start_block, count_blocks, 0).astype(jnp.float32)
    return jnp.repeat(live, width)


def one_supernode(inverse_rows, masked, mask_cols, diag_part, source_col):
    partial_value = jnp.dot(
        inverse_rows, masked, precision=lax.Precision.HIGHEST, preferred_element_type=jnp.float32
    )
    column_total = lax.psum(partial_value, "row")
    column = -(mask_cols[:, None] * column_total)
    lower = from_root(column, "col", source_col)
    inner = jnp.dot(
        masked.T, lower, precision=lax.Precision.HIGHEST, preferred_element_type=jnp.float32
    )
    diagonal = diag_part - lax.psum(inner, "row")
    return (lower, column.T, diagonal)


def shards(inverse_rows, panels, diag_inverse, pattern, owner_slot):
    n_rows = lax.axis_size("row")
    n_cols = lax.axis_size("col")
    row_index = lax.axis_index("row")
    col_index = lax.axis_index("col")
    width = panels.shape[2]
    blocks = pattern.shape[1]
    source_col = row_index * n_cols // n_rows
    masked_list = []
    colmask_list = []
    for number in range(2):
        mask_rows = block_mask(
            pattern[number], row_index * (blocks // n_rows), blocks // n_rows, width
        )
        mask_cols = block_mask(
            pattern[number], col_index * (blocks // n_cols), blocks // n_cols, width
        )
        held = from_root(panels[0], "col", owner_slot[number])
        masked_list.append(mask_rows[:, None] * held)
        colmask_list.append(mask_cols)
    lowers = []
    uppers = []
    diagonals = []
    for number in range(2):
        lower, upper, diagonal = one_supernode(
            inverse_rows,
            masked_list[number],
            colmask_list[number],
            diag_inverse[number],
            source_col,
        )
        lowers.append(lower)
        uppers.append(upper)
        diagonals.append(diagonal)
    return (jnp.stack(lowers), jnp.stack(uppers), jnp.stack(diagonals))


def solution(mesh):
    in_specs = (P("col", "row"), P("col", "row", None), P(), P(), P())
    out_specs = (P(None, "row", None), P(None, None, "col"), P())
    return jax.shard_map(shards, mesh=mesh, in_specs=in_specs, out_specs=out_specs, check_vma=False)
```

profile of v0, /device:TPU:2, one launch (start us, length us, event | category | flops | bytes accessed | tf_op | source)
XLA Modules:
  0.0 634.4 jit_solution(743033753647602464)
XLA Ops:
  7.2 0.0 all-reduce.11.cloned.1.call-start
  7.2 1.3 fusion.25
  9.8 0.0 copy-start.8
  9.8 2.7 select_bitcast_fusion.1
  12.5 0.0 all-reduce.11.cloned.1.call-update
  12.6 0.0 all-reduce.15.cloned.1.call-start
  12.6 0.0 copy-done.8
  12.6 0.1 fusion.17
  12.7 0.1 broadcast_bitcast_fusion.2
  12.8 0.1 broadcast_bitcast_fusion
  12.9 169.4 %all-reduce.11.cloned.1.call-done = (f32[1024,256]{1,0:T(8,128)}, f32[1024,256]{1,0:T(8,128)}) async-done(((f32[1024,256]{1,0:T(8,128)}, f32[1024,256]{1,0:T(8,128)}), (f32[1024,256]{1,0:T(8,128)}, f32[1024,256]{1,0:T(8,128)})) %all-reduce.11.cloned.1.call-update) | async-done | bytes 2097168 | tf_op jit(solution)/shard_map/psum | solution.py:9
  182.3 0.0 copy-start
  182.3 0.0 copy-start.2
  182.3 10.6 %convolution_bitcast_fusion = f32[1024,256]{0,1:T(8,128)} fusion(f32[1024,1024]{1,0:T(8,128)} %param.5, f32[1024,256]{1,0:T(8,128)} %get-tuple-element.8, f32[1024]{0:T(1024)S(1)} %bitcast.60), kind=kOutput, calls=%fused_computation.2 | convolution fusion | flops 3221487616 | bytes 6295552 | tf_op jit(solution)/shard_map/dot_general | solution.py:18
  192.9 0.0 copy-done
  192.9 0.0 copy-done.2
  192.9 8.2 %convolution_bitcast_fusion.1 = f32[1024,256]{0,1:T(8,128)} fusion(f32[1024,1024]{1,0:T(8,128)S(1)} %copy-done, f32[1024,256]{1,0:T(8,128)S(1)} %copy-done.2, f32[1024]{0:T(1024)S(1)} %bitcast.58), kind=kOutput, calls=%fused_computation.3 | convolution fusion | flops 3221487616 | bytes 6295552 | tf_op jit(solution)/shard_map/dot_general | solution.py:18
  201.1 0.0 all-reduce.15.cloned.1.call-update
  201.2 0.0 all-reduce.9.cloned.1.call-start
  201.2 0.1 broadcast_bitcast_fusion.3
  201.3 0.1 broadcast_bitcast_fusion.1
  201.4 125.1 %all-reduce.15.cloned.1.call-done = (f32[1024,256]{0,1:T(8,128)}, f32[1024,256]{0,1:T(8,128)}) async-done(((f32[1024,256]{0,1:T(8,128)}, f32[1024,256]{0,1:T(8,128)}), (f32[1024,256]{0,1:T(8,128)}, f32[1024,256]{0,1:T(8,128)})) %all-reduce.15.cloned.1.call-update) | async-done | bytes 2097168 | tf_op jit(solution)/shard_map/psum | solution.py:21
  326.5 0.0 copy-start.6
  326.5 2.9 fusion.8
  329.4 0.0 copy-done.6
  329.4 1.6 fusion.6
  331.0 0.0 copy-start.1
  331.0 0.0 all-reduce.9.cloned.1.call-update
  331.0 0.0 all-reduce.13.cloned.1.call-start
  331.1 170.1 %all-reduce.9.cloned.1.call-done = (f32[1024,256]{0,1:T(8,128)}, f32[1024,256]{0,1:T(8,128)}) async-done(((f32[1024,256]{0,1:T(8,128)}, f32[1024,256]{0,1:T(8,128)}), (f32[1024,256]{0,1:T(8,128)}, f32[1024,256]{0,1:T(8,128)})) %all-reduce.9.cloned.1.call-update) | async-done | bytes 2097168 | tf_op jit(solution)/shard_map/psum | solution.py:9
  501.2 0.0 copy-start.3
  501.2 4.0 fusion.3
  505.2 0.0 copy-start.5
  505.2 0.0 copy-done.1
  505.2 0.0 copy-done.3
  505.2 2.7 fusion
  507.9 0.0 all-reduce.13.cloned.1.call-update
  508.0 0.0 copy-done.5
  508.0 0.0 copy-start.4
  508.0 2.8 pad_maximum_fusion.1
  510.8 0.0 copy-done.4
  510.8 0.2 pad_maximum_fusion
  511.1 0.0 copy-start.7
  511.1 1.8 copy.8
  512.9 113.1 %all-reduce.13.cloned.1.call-done = (f32[256,256]{1,0:T(8,128)}, f32[256,256]{1,0:T(8,128)}) async-done(((f32[256,256]{1,0:T(8,128)}, f32[256,256]{1,0:T(8,128)}), (f32[256,256]{1,0:T(8,128)}, f32[256,256]{1,0:T(8,128)})) %all-reduce.13.cloned.1.call-update) | async-done | bytes 524304 | tf_op jit(solution)/shard_map/psum | solution.py:27
  625.9 0.0 copy-done.7
  626.0 1.1 fusion.15
  627.0 0.8 pad_maximum_fusion.2
  (5 shorter events, 0.0 us)
Async XLA Ops:
  7.2 175.1 %all-reduce.11.cloned.1.call-start = ((), (), s32[]{:S(2)}) async-start(), calls=%async_computation.1 | async-start | bytes 4194304 | tf_op jit(solution)/shard_map/psum | solution.py:9
  9.8 2.8 copy-start.8
  12.6 313.9 %all-reduce.15.cloned.1.call-start = ((), (), s32[]{:S(2)}) async-start(), calls=%async_computation.3 | async-start | bytes 4194304 | tf_op jit(solution)/shard_map/psum | solution.py:21
  182.3 10.6 %copy-start = (f32[1024,1024]{1,0:T(8,128)S(1)}, f32[1024,1024]{1,0:T(8,128)}, u32[]{:S(2)}) copy-start(f32[1024,1024]{1,0:T(8,128)} %param.5) | copy-start | bytes 12582916
  182.3 10.6 %copy-start.2 = (f32[1024,256]{1,0:T(8,128)S(1)}, f32[1024,256]{1,0:T(8,128)}, u32[]{:S(2)}) copy-start(f32[1024,256]{1,0:T(8,128)} %get-tuple-element.9) | copy-start | bytes 3145732
  201.2 300.0 %all-reduce.9.cloned.1.call-start = ((), (), s32[]{:S(2)}) async-start(), calls=%async_computation | async-start | bytes 4194304 | tf_op jit(solution)/shard_map/psum | solution.py:9
  326.5 2.9 copy-start.6
  331.0 174.2 %copy-start.1 = (f32[1024,256]{1,0:T(8,128)S(1)}, f32[1024,256]{1,0:T(8,128)}, u32[]{:S(2)}) copy-start(f32[1024,256]{1,0:T(8,128)} %get-tuple-element.8) | copy-start | bytes 3145732
  331.0 294.9 %all-reduce.13.cloned.1.call-start = ((), (), s32[]{:S(2)}) async-start(), calls=%async_computation.2 | async-start | bytes 1048576 | tf_op jit(solution)/shard_map/psum | solution.py:27
  501.2 4.0 copy-start.3
  505.2 2.7 copy-start.5
  508.0 2.8 copy-start.4
  511.1 114.9 %copy-start.7 = (f32[2,256,256]{2,1,0:T(8,128)S(1)}, f32[2,256,256]{2,1,0:T(8,128)}, u32[]{:S(2)}) copy-start(f32[2,256,256]{2,1,0:T(8,128)} %param.7) | copy-start | bytes 1572868
Sparse Core Ops, SparseCore 0:
  12.7 169.5 all-reduce.10
  201.3 125.1 all-reduce.14
  331.2 169.9 all-reduce.8
  508.1 117.8 all-reduce.12
where the time goes:
time: 639 us; the launch traced here: 634 us
  waiting for transfers between devices  578 us (90%)
  matrix products  25.6 us (4%)
  between operations  15.2 us (2%)
  other arithmetic  12.3 us (2%)
    psum x2, waiting for transfers between devices, from_root(): return lax.psum(jnp.where(mine, array, jnp.zeros_like(array)), axis)  340 us
    psum x1, waiting for transfers between devices, one_supernode(): column_total = lax.psum(partial_value, 'row')  125 us
    psum x1, waiting for transfers between devices, one_supernode(): diagonal = diag_part - lax.psum(inner, 'row')  113 us
    dot_general x2, matrix products, one_supernode(): jnp.dot(inverse_rows, masked, precision=lax.Precision.HIGHEST, preferred_...  18.8 us
  transfers between devices with their start and end apart: 4, of which 4 were waited for; matrix products, arithmetic and copies ran while one was open for 1% of the time, Pallas kernels for 0%

commit v1 on v0

v1 whole, which is shorter than its diff:
```python
import jax
import jax.numpy as jnp
import numpy as np
from jax import lax
from jax.sharding import Mesh
from jax.sharding import PartitionSpec as P

SIZES = {"y": 4, "xl": 2, "core": 2, "z": 8, "xh": 2}
ROW = ("y", "xl", "core")
CHIP = ("y", "xl")
COL = ("z", "xh")
ALL = ROW + COL


def swap_pairs():
    return [(0, 1), (1, 0)]


def turn_pairs(step):
    n = SIZES["z"]
    return [(i, (i + step) % n) for i in range(n)]


def transpose_pairs():
    return [(r * 16 + c, c * 16 + r) for r in range(16) for c in range(16)]


def both(mine, other, first):
    return jnp.where(first, jnp.stack([mine, other]), jnp.stack([other, mine]))


def ring(block, axis_dim):
    z = lax.axis_index("z")
    n = SIZES["z"]
    half = block.shape[-2] // 2
    shape = block.shape[:axis_dim] + (n,) + block.shape[axis_dim:]
    out = jnp.zeros(shape, block.dtype)

    def put(out, piece, index, row):
        start = [0] * len(shape)
        start[axis_dim] = index % n
        start[-2] = row
        return lax.dynamic_update_slice(out, jnp.expand_dims(piece, axis_dim), start)

    out = put(out, block, z, 0)
    up = down = block
    for k in range(1, 4):
        up = lax.ppermute(up, "z", turn_pairs(1))
        down = lax.ppermute(down, "z", turn_pairs(-1))
        out = put(out, up, z - k + n, 0)
        out = put(out, down, z + k, 0)
    up = lax.ppermute(up[..., :half, :], "z", turn_pairs(1))
    down = lax.ppermute(down[..., half:, :], "z", turn_pairs(-1))
    out = put(out, up, z + 4, 0)
    out = put(out, down, z + 4, half)
    return out


def dot(a, b):
    return jnp.dot(a, b, precision=lax.Precision.HIGH, preferred_element_type=jnp.float32)


def shards(inverse_rows, panels, diag_inverse, pattern, owner_slot):
    row = lax.axis_index(ROW)
    col = lax.axis_index(COL)
    chip = lax.axis_index(CHIP)
    core = lax.axis_index("core")
    xh = lax.axis_index("xh")
    live = pattern.astype(jnp.float32)

    dealt = lax.all_to_all(panels[0].reshape(16, 64, 256), COL, 0, 0, tiled=True)
    mask = lax.dynamic_slice_in_dim(live, row * 4 + col // 4, 1, 1)[:, :, None]
    chunk = mask * jnp.stack(
        [lax.dynamic_index_in_dim(dealt, owner_slot[s], 0, keepdims=False) for s in range(2)]
    )
    chunk = jnp.concatenate([chunk[0], chunk[1]], axis=1)
    other = lax.ppermute(chunk, "xh", swap_pairs())
    block = both(chunk, other, xh == 0).reshape(128, 512)
    masked = ring(block, 0).reshape(1024, 512)

    first = core == 0
    send_in = jnp.where(first, masked[:, 256:], masked[:, :256])
    keep_in = jnp.where(first, masked[:, :256], masked[:, 256:])
    received = lax.ppermute(dot(inverse_rows, send_in), "core", swap_pairs())
    term = dot(inverse_rows, keep_in) + received
    terms = lax.all_to_all(term.reshape(8, 128, 256), CHIP, 0, 0, tiled=True)
    total = jnp.sum(terms, axis=0)
    mask = lax.dynamic_slice(live, (core, col * 4 + chip // 2), (1, 1))
    column = -(mask * total)

    rows = lax.all_gather(column.T, ROW, axis=0, tiled=False)
    rows = rows.reshape(8, 2, 256, 128).transpose(1, 2, 0, 3).reshape(2, 256, 1024)

    other = lax.ppermute(column, "core", swap_pairs())
    pair = both(column, other, first)
    pair = lax.ppermute(pair, ALL, transpose_pairs())
    lower = ring(pair, 1).reshape(2, 1024, 256)

    left = jnp.where(xh == 0, block[:, :256], block[:, 256:])
    right = jnp.where(xh == 0, pair[0], pair[1])
    inner = dot(left.T, right)
    inner = jnp.sum(lax.all_to_all(inner.reshape(16, 16, 256), ROW, 0, 0, tiled=True), axis=0)
    spread = jnp.broadcast_to(inner[None], (8, 16, 256))
    inner = jnp.sum(lax.all_to_all(spread, "z", 0, 0, tiled=True), axis=0)
    spread = jnp.broadcast_to(inner[None], (32, 16, 256))
    inner = lax.all_to_all(spread, ROW + ("xh",), 0, 0, tiled=True)
    inner = inner.reshape(16, 2, 16, 256).transpose(1, 0, 2, 3).reshape(2, 256, 256)
    return lower, rows, diag_inverse - inner


def solution(mesh):
    fine = Mesh(np.asarray(mesh.devices).reshape(4, 2, 2, 8, 2), ALL)
    in_specs = (P(COL, ROW), P(COL, ROW, None), P(), P(), P())
    out_specs = (P(None, ROW, None), P(None, None, COL), P())
    return jax.shard_map(shards, mesh=fine, in_specs=in_specs, out_specs=out_specs, check_vma=False)
```

time: 639 us -> 229 us (0.36)
  waiting for transfers between devices: 578 us -> 113 us
  starting transfers between devices: 0.16 us -> 68.9 us
  matrix products: 25.6 us -> 8.32 us
  local copies, waits for them, and re-layouts: 3.48 us -> 15.1 us
  other arithmetic: 12.3 us -> 3.76 us
    psum x4 -> x0, waiting for transfers between devices: 578 us -> none  [the longest x2 340 us: from_root(): return lax.psum(jnp.where(mine, array, jnp.zeros_like(array)), axis)]
    ppermute x0 -> x20, waiting for transfers between devices: none -> 60.6 us  [the longest x1 22.5 us: shards(): pair = lax.ppermute(pair, ALL, transpose_pairs())]
    all_to_all x0 -> x5, waiting for transfers between devices: none -> 52.9 us  [the longest x1 25.4 us: shards(): lax.all_to_all(panels[0].reshape(16, 64, 256), COL, 0, 0, tiled=True)]
    all_to_all x0 -> x5, starting transfers between devices: none -> 37.2 us  [the longest x1 12.9 us: shards(): lax.all_to_all(inner.reshape(16, 16, 256), ROW, 0, 0, tiled=True)]
    ppermute x0 -> x20, starting transfers between devices: none -> 31.7 us  [the longest x6 19.6 us: ring(): down = lax.ppermute(down, 'z', turn_pairs(-1))]
    dot_general x4 -> x3, matrix products: 25.6 us -> 8.32 us  [dot(): jnp.dot(a, b, precision=lax.Precision.HIGH, preferred_element_type=jnp.fl...]
    another operation x6 -> x1, other arithmetic: 9.51 us -> 0.02 us  [both(): return jnp.where(first, jnp.stack([mine, other]), jnp.stack([other, mine]))]
  transfers between devices with their start and end apart: 4 -> 26, of which waited for: 4 -> 14; matrix products, arithmetic and copies ran while one was open for 1% -> 6% of each run, Pallas kernels for 0% -> 0%
where the time goes in v1:
time: 229 us; the launch traced here: 228 us
  waiting for transfers between devices  113 us (49%)
  starting transfers between devices  68.9 us (30%)
  between operations  18.4 us (8%)
  local copies, waits for them, and re-layouts  15.1 us (7%)
  matrix products  8.32 us (4%)
  other arithmetic  3.76 us (2%)
    all_to_all x1, waiting for transfers between devices, shards(): lax.all_to_all(panels[0].reshape(16, 64, 256), COL, 0, 0, tiled=True)  25.4 us
    ppermute x1, waiting for transfers between devices, shards(): pair = lax.ppermute(pair, ALL, transpose_pairs())  22.5 us
    ppermute x6, waiting for transfers between devices, ring(): up = lax.ppermute(up, 'z', turn_pairs(1))  21.4 us
    ppermute x6, starting transfers between devices, ring(): down = lax.ppermute(down, 'z', turn_pairs(-1))  19.6 us
    all_to_all x1, waiting for transfers between devices, shards(): terms = lax.all_to_all(term.reshape(8, 128, 256), CHIP, 0, 0, tiled=True)  14.3 us
    all_to_all x1, starting transfers between devices, shards(): lax.all_to_all(inner.reshape(16, 16, 256), ROW, 0, 0, tiled=True)  12.9 us
    all_to_all x1, starting transfers between devices, shards(): lax.all_to_all(panels[0].reshape(16, 64, 256), COL, 0, 0, tiled=True)  10.3 us
    dot_general x3, matrix products, dot(): jnp.dot(a, b, precision=lax.Precision.HIGH, preferred_element_type=jnp.fl...  8.32 us
  transfers between devices with their start and end apart: 26, of which 14 were waited for; matrix products, arithmetic and copies ran while one was open for 6% of the time, Pallas kernels for 0%

profile of v1, /device:TPU:2, one launch (start us, length us, event | category | flops | bytes accessed | tf_op | source)
XLA Modules:
  0.0 227.9 jit_solution(11761991877243272270)
XLA Ops:
  7.2 10.3 %all-to-all-start = ((f32[16,64,256]{2,1,0:T(8,128)}), f32[16,64,256]{2,1,0:T(8,128)S(1)}, u32[]{:S(2)}, u32[]{:S(2)}) async-start(f32[16,64,256]{2,1,0:T(8,128)} %bitcast.101), calls=%async_computation | async-start | bytes 2097152 | tf_op jit(solution)/shard_map/all_to_all | solution.py:71
  22.2 25.4 %all-to-all-done = f32[16,64,256]{2,1,0:T(8,128)S(1)} async-done(((f32[16,64,256]{2,1,0:T(8,128)}), f32[16,64,256]{2,1,0:T(8,128)S(1)}, u32[]{:S(2)}, u32[]{:S(2)}) %all-to-all-start) | async-done | bytes 1048608 | tf_op jit(solution)/shard_map/all_to_all | solution.py:71
  48.3 6.0 %collective-permute-done = f32[64,512]{1,0:T(8,128)S(1)} collective-permute-done((f32[64,512]{1,0:T(8,128)S(1)}, f32[64,512]{1,0:T(8,128)S(1)}, u32[]{:S(2)}, u32[]{:S(2)}) %collective-permute-start) | collective-permute-done | bytes 131104 | tf_op jit(solution)/shard_map/ppermute | solution.py:77
  54.5 3.2 %collective-permute-start.2 = (f32[128,512]{1,0:T(8,128)S(1)}, f32[128,512]{1,0:T(8,128)S(1)}, u32[]{:S(2)}, u32[]{:S(2)}) collective-permute-start(f32[128,512]{1,0:T(8,128)S(1)} %bitcast.94), channel_id=1, source_target_pairs={{0,14},{2,0},{4,2},{6,4},{8,6},{10,8},{12,10},{14,12},{1,15},{3,1}... | collective-permute-start | bytes 786440 | tf_op jit(solution)/shard_map/ppermute | solution.py:49
  58.0 6.4 %collective-permute-done.1 = f32[128,512]{1,0:T(8,128)S(1)} collective-permute-done((f32[128,512]{1,0:T(8,128)S(1)}, f32[128,512]{1,0:T(8,128)S(1)}, u32[]{:S(2)}, u32[]{:S(2)}) %collective-permute-start.1) | collective-permute-done | bytes 262176 | tf_op jit(solution)/shard_map/ppermute | solution.py:48
  64.4 3.4 %collective-permute-start.4 = (f32[128,512]{1,0:T(8,128)S(1)}, f32[128,512]{1,0:T(8,128)S(1)}, u32[]{:S(2)}, u32[]{:S(2)}) collective-permute-start(f32[128,512]{1,0:T(8,128)S(1)} %collective-permute-done.2), channel_id=1, source_target_pairs={{0,14},{2,0},{4,2},{6,4},{8,6},{10,8},{12,10},{14,12},{1,15},{3,1}... | collective-permute-start | bytes 786440 | tf_op jit(solution)/shard_map/ppermute | solution.py:49
  67.9 6.2 %collective-permute-done.3 = f32[128,512]{1,0:T(8,128)S(1)} collective-permute-done((f32[128,512]{1,0:T(8,128)S(1)}, f32[128,512]{1,0:T(8,128)S(1)}, u32[]{:S(2)}, u32[]{:S(2)}) %collective-permute-start.3) | collective-permute-done | bytes 262176 | tf_op jit(solution)/shard_map/ppermute | solution.py:48
  74.1 3.3 %collective-permute-start.6 = (f32[128,512]{1,0:T(8,128)S(1)}, f32[128,512]{1,0:T(8,128)S(1)}, u32[]{:S(2)}, u32[]{:S(2)}) collective-permute-start(f32[128,512]{1,0:T(8,128)S(1)} %collective-permute-done.4), channel_id=1, source_target_pairs={{0,14},{2,0},{4,2},{6,4},{8,6},{10,8},{12,10},{14,12},{1,15},{3,1}... | collective-permute-start | bytes 786440 | tf_op jit(solution)/shard_map/ppermute | solution.py:49
  77.5 4.2 %collective-permute-done.5 = f32[128,512]{1,0:T(8,128)S(1)} collective-permute-done((f32[128,512]{1,0:T(8,128)S(1)}, f32[128,512]{1,0:T(8,128)S(1)}, u32[]{:S(2)}, u32[]{:S(2)}) %collective-permute-start.5) | collective-permute-done | bytes 262176 | tf_op jit(solution)/shard_map/ppermute | solution.py:48
  81.8 3.3 %collective-permute-start.8 = (f32[64,512]{1,0:T(8,128)S(1)}, f32[64,512]{1,0:T(8,128)S(1)}, u32[]{:S(2)}, u32[]{:S(2)}) collective-permute-start(f32[64,512]{1,0:T(8,128)S(1)} %slice.61), channel_id=1, source_target_pairs={{0,14},{2,0},{4,2},{6,4},{8,6},{10,8},{12,10},{14,12},{1,15},{3,1}... | collective-permute-start | bytes 393224 | tf_op jit(solution)/shard_map/ppermute | solution.py:53
  85.1 2.8 %collective-permute-done.7 = f32[64,512]{1,0:T(8,128)S(1)} collective-permute-done((f32[64,512]{1,0:T(8,128)S(1)}, f32[64,512]{1,0:T(8,128)S(1)}, u32[]{:S(2)}, u32[]{:S(2)}) %collective-permute-start.7) | collective-permute-done | bytes 131104 | tf_op jit(solution)/shard_map/ppermute | solution.py:52
  88.0 3.7 %convolution_bitcast_fusion = f32[1024,256]{0,1:T(8,128)S(1)} fusion(f32[1024,1024]{1,0:T(8,128)S(1)} %copy-done, f32[1024,512]{1,0:T(8,128)S(1)} %bitcast.91, pred[]{:T(512)S(6)} %eq.27), kind=kOutput, calls=%fused_computation.1 | convolution fusion | flops 1610874880 | bytes 7340033 | tf_op jit(solution)/shard_map/dot_general | solution.py:60
  91.9 2.6 %collective-permute-done.9 = f32[1024,256]{0,1:T(8,128)S(1)} collective-permute-done((f32[1024,256]{0,1:T(8,128)S(1)}, f32[1024,256]{0,1:T(8,128)S(1)}, u32[]{:S(2)}, u32[]{:S(2)}) %collective-permute-start.9) | collective-permute-done | bytes 1048608 | tf_op jit(solution)/shard_map/ppermute | solution.py:84
  94.6 3.7 %fusion.1 = f32[32,8,8,128]{3,2,1,0:T(8,128)S(1)} fusion(f32[1024,256]{0,1:T(8,128)S(1)} %collective-permute-done.9, f32[1024,1024]{1,0:T(8,128)S(1)} %copy-done, f32[1024,512]{1,0:T(8,128)S(1)} %bitcast.92, pred[]{:T(512)S(6)} %eq.27), kind=kOutput, calls=%fused_computation.4 | convolution fusion | flops 1611137024 | bytes 8388609 | tf_op jit(solution)/shard_map/dot_general | solution.py:60
  98.3 1.0 copy.73
  99.3 5.9 %all-to-all-start.1 = ((f32[8,128,256]{1,2,0:T(8,128)}), f32[8,128,256]{1,2,0:T(8,128)S(1)}, u32[]{:S(2)}, u32[]{:S(2)}) async-start(f32[8,128,256]{1,2,0:T(8,128)} %bitcast.88), calls=%async_computation.1 | async-start | bytes 2097152 | tf_op jit(solution)/shard_map/all_to_all | solution.py:86
  105.8 14.3 %all-to-all-done.1 = f32[8,128,256]{1,2,0:T(8,128)S(1)} async-done(((f32[8,128,256]{1,2,0:T(8,128)}), f32[8,128,256]{1,2,0:T(8,128)S(1)}, u32[]{:S(2)}, u32[]{:S(2)}) %all-to-all-start.1) | async-done | bytes 1048608 | tf_op jit(solution)/shard_map/all_to_all | solution.py:86
  120.1 1.3 fusion.22
  121.5 0.7 multiply_negate_fusion
  122.3 0.7 fusion.23
  122.9 0.7 collective-permute-done.10
  123.6 1.9 collective-permute-start.11
  125.8 22.5 %collective-permute-done.11 = f32[2,128,256]{1,2,0:T(8,128)S(1)} collective-permute-done((f32[2,128,256]{1,2,0:T(8,128)S(1)}, f32[2,128,256]{1,2,0:T(8,128)S(1)}, u32[]{:S(2)}, u32[]{:S(2)}) %collective-permute-start.11) | collective-permute-done | bytes 262176 | tf_op jit(solution)/shard_map/ppermute | solution.py:96
  148.2 5.5 %collective-permute-start.13 = (f32[2,128,256]{1,2,0:T(8,128)S(1)}, f32[2,128,256]{1,2,0:T(8,128)S(1)}, u32[]{:S(2)}, u32[]{:S(2)}) collective-permute-start(f32[2,128,256]{1,2,0:T(8,128)S(1)} %collective-permute-done.11), channel_id=1, source_target_pairs={{0,14},{2,0},{4,2},{6,4},{8,6},{10,8},{12,10},{14,12},{1,15},{3,1}... | collective-permute-start | bytes 786440 | tf_op jit(solution)/shard_map/ppermute | solution.py:49
  153.8 1.0 fusion.11
  154.8 12.9 %all-to-all-start.2 = ((f32[16,16,256]{2,1,0:T(8,128)}), f32[16,16,256]{2,1,0:T(8,128)S(1)}, u32[]{:S(2)}, u32[]{:S(2)}) async-start(f32[16,16,256]{2,1,0:T(8,128)} %fusion.11), calls=%async_computation.2 | async-start | bytes 524288 | tf_op jit(solution)/shard_map/all_to_all | solution.py:102
  167.9 6.6 %all-to-all-done.2 = f32[16,16,256]{2,1,0:T(8,128)S(1)} async-done(((f32[16,16,256]{2,1,0:T(8,128)}), f32[16,16,256]{2,1,0:T(8,128)S(1)}, u32[]{:S(2)}, u32[]{:S(2)}) %all-to-all-start.2) | async-done | bytes 262176 | tf_op jit(solution)/shard_map/all_to_all | solution.py:102
  174.5 0.7 broadcast_in_dim.89
  175.2 3.4 %all-to-all-start.3 = ((f32[8,16,256]{2,1,0:T(8,128)}), f32[8,16,256]{2,1,0:T(8,128)S(1)}, u32[]{:S(2)}, u32[]{:S(2)}) async-start(f32[8,16,256]{2,1,0:T(8,128)} %broadcast_in_dim.89), calls=%async_computation.3 | async-start | bytes 262144 | tf_op jit(solution)/shard_map/all_to_all | solution.py:104
  178.5 1.9 collective-permute-start.14
  180.5 1.4 collective-permute-start.15
  181.9 6.6 %all-to-all-done.3 = f32[8,16,256]{2,1,0:T(8,128)S(1)} async-done(((f32[8,16,256]{2,1,0:T(8,128)}), f32[8,16,256]{2,1,0:T(8,128)S(1)}, u32[]{:S(2)}, u32[]{:S(2)}) %all-to-all-start.3) | async-done | bytes 131104 | tf_op jit(solution)/shard_map/all_to_all | solution.py:104
  188.5 0.9 broadcast_in_dim.90
  189.4 4.8 %all-to-all-start.4 = ((f32[32,16,256]{2,1,0:T(8,128)}), f32[32,16,256]{2,1,0:T(8,128)S(1)}, u32[]{:S(2)}, u32[]{:S(2)}) async-start(f32[32,16,256]{2,1,0:T(8,128)} %broadcast_in_dim.90), calls=%async_computation.4 | async-start | bytes 1048576 | tf_op jit(solution)/shard_map/all_to_all | solution.py:106
  194.2 0.6 collective-permute-start.16
  194.8 2.7 %collective-permute-start.17 = (f32[2,128,256]{1,2,0:T(8,128)}, f32[2,128,256]{1,2,0:T(8,128)S(1)}, u32[]{:S(2)}, u32[]{:S(2)}) collective-permute-start(f32[2,128,256]{1,2,0:T(8,128)} %collective-permute-done.15), channel_id=1, source_target_pairs={{0,14},{2,0},{4,2},{6,4},{8,6},{10,8},{12,10},{14,12},{1,15},{3,1}... | collective-permute-start | bytes 786440 | tf_op jit(solution)/shard_map/ppermute | solution.py:49
  197.5 1.0 bitcast_dynamic-update-slice_fusion.3
  198.5 1.0 bitcast_dynamic-update-slice_fusion.2
  199.4 4.6 %collective-permute-done.16 = f32[2,128,256]{1,2,0:T(8,128)S(1)} collective-permute-done((f32[2,128,256]{1,2,0:T(8,128)}, f32[2,128,256]{1,2,0:T(8,128)S(1)}, u32[]{:S(2)}, u32[]{:S(2)}) %collective-permute-start.16) | collective-permute-done | bytes 262176 | tf_op jit(solution)/shard_map/ppermute | solution.py:48
  204.0 0.8 slice.65
  204.9 3.2 %collective-permute-start.19 = (f32[2,64,256]{1,2,0:T(8,128)}, f32[2,64,256]{1,2,0:T(8,128)}, u32[]{:S(2)}, u32[]{:S(2)}) collective-permute-start(f32[2,64,256]{1,2,0:T(8,128)} %slice.65), channel_id=1, source_target_pairs={{0,14},{2,0},{4,2},{6,4},{8,6},{10,8},{12,10},{14,12},{1,15},{3,1}... | collective-permute-start | bytes 393224 | tf_op jit(solution)/shard_map/ppermute | solution.py:53
  208.2 4.6 %collective-permute-done.18 = f32[2,64,256]{1,2,0:T(8,128)S(1)} collective-permute-done((f32[2,64,256]{1,2,0:T(8,128)S(1)}, f32[2,64,256]{1,2,0:T(8,128)S(1)}, u32[]{:S(2)}, u32[]{:S(2)}) %collective-permute-start.18) | collective-permute-done | bytes 131104 | tf_op jit(solution)/shard_map/ppermute | solution.py:52
  212.8 0.6 dynamic_update_slice.70
  213.4 1.8 copy.56
  215.2 1.1 copy.57
  216.3 0.7 constant_dynamic-update-slice_fusion
  217.0 0.9 bitcast_subtract_fusion
  217.9 3.2 %copy.72 = f32[8,2,32,8,128]{4,3,0,2,1:T(8,128)} copy(f32[8,2,32,8,128]{4,3,2,1,0:T(8,128)} %bitcast.97) | data formatting | bytes 4194304 | tf_op jit(solution)/shard_map/reshape | solution.py:92
  (67 shorter events, 3.8 us)
Async XLA Ops:
  7.2 10.3 %copy-start.2 = (s32[2]{0:T(128)S(1)}, s32[2]{0:T(128)}, u32[]{:S(2)}) copy-start(s32[2]{0:T(128)} %param.9) | copy-start | bytes 28
  7.2 13.5 %copy-start.3 = (s32[2,64]{1,0:T(2,128)S(1)}, s32[2,64]{1,0:T(2,128)}, u32[]{:S(2)}) copy-start(s32[2,64]{1,0:T(2,128)} %param.8) | copy-start | bytes 1540
  7.2 40.5 %all-to-all-start = ((f32[16,64,256]{2,1,0:T(8,128)}), f32[16,64,256]{2,1,0:T(8,128)S(1)}, u32[]{:S(2)}, u32[]{:S(2)}) async-start(f32[16,64,256]{2,1,0:T(8,128)} %bitcast.101), calls=%async_computation | async-start | bytes 2097152 | tf_op jit(solution)/shard_map/all_to_all | solution.py:71
  47.8 6.6 %collective-permute-start = (f32[64,512]{1,0:T(8,128)S(1)}, f32[64,512]{1,0:T(8,128)S(1)}, u32[]{:S(2)}, u32[]{:S(2)}) collective-permute-start(f32[64,512]{1,0:T(8,128)S(1)} %get-tuple-element.8), channel_id=1, source_target_pairs={{0,1},{1,0},{2,3},{3,2},{4,5},{5,4},{6,7},{7,6},{8,9},{9,8},{10,11... | collective-permute-start | bytes 393224 | tf_op jit(solution)/shard_map/ppermute | solution.py:77
  54.4 10.0 %collective-permute-start.1 = (f32[128,512]{1,0:T(8,128)S(1)}, f32[128,512]{1,0:T(8,128)S(1)}, u32[]{:S(2)}, u32[]{:S(2)}) collective-permute-start(f32[128,512]{1,0:T(8,128)S(1)} %bitcast.93), channel_id=1, source_target_pairs={{0,2},{2,4},{4,6},{6,8},{8,10},{10,12},{12,14},{14,0},{1,3},{3,5},... | collective-permute-start | bytes 786440 | tf_op jit(solution)/shard_map/ppermute | solution.py:48
  54.5 10.0 %collective-permute-start.2 = (f32[128,512]{1,0:T(8,128)S(1)}, f32[128,512]{1,0:T(8,128)S(1)}, u32[]{:S(2)}, u32[]{:S(2)}) collective-permute-start(f32[128,512]{1,0:T(8,128)S(1)} %bitcast.94), channel_id=1, source_target_pairs={{0,14},{2,0},{4,2},{6,4},{8,6},{10,8},{12,10},{14,12},{1,15},{3,1}... | collective-permute-start | bytes 786440 | tf_op jit(solution)/shard_map/ppermute | solution.py:49
  58.0 30.0 %copy-start = (f32[1024,1024]{1,0:T(8,128)S(1)}, f32[1024,1024]{1,0:T(8,128)}, u32[]{:S(2)}) copy-start(f32[1024,1024]{1,0:T(8,128)} %param.5) | copy-start | bytes 12582916
  64.4 9.7 %collective-permute-start.3 = (f32[128,512]{1,0:T(8,128)S(1)}, f32[128,512]{1,0:T(8,128)S(1)}, u32[]{:S(2)}, u32[]{:S(2)}) collective-permute-start(f32[128,512]{1,0:T(8,128)S(1)} %collective-permute-done.1), channel_id=1, source_target_pairs={{0,2},{2,4},{4,6},{6,8},{8,10},{10,12},{12,14},{14,0},{1,3},{3,5},... | collective-permute-start | bytes 786440 | tf_op jit(solution)/shard_map/ppermute | solution.py:48
  64.4 9.7 %collective-permute-start.4 = (f32[128,512]{1,0:T(8,128)S(1)}, f32[128,512]{1,0:T(8,128)S(1)}, u32[]{:S(2)}, u32[]{:S(2)}) collective-permute-start(f32[128,512]{1,0:T(8,128)S(1)} %collective-permute-done.2), channel_id=1, source_target_pairs={{0,14},{2,0},{4,2},{6,4},{8,6},{10,8},{12,10},{14,12},{1,15},{3,1}... | collective-permute-start | bytes 786440 | tf_op jit(solution)/shard_map/ppermute | solution.py:49
  74.1 7.6 %collective-permute-start.5 = (f32[128,512]{1,0:T(8,128)S(1)}, f32[128,512]{1,0:T(8,128)S(1)}, u32[]{:S(2)}, u32[]{:S(2)}) collective-permute-start(f32[128,512]{1,0:T(8,128)S(1)} %collective-permute-done.3), channel_id=1, source_target_pairs={{0,2},{2,4},{4,6},{6,8},{8,10},{10,12},{12,14},{14,0},{1,3},{3,5},... | collective-permute-start | bytes 786440 | tf_op jit(solution)/shard_map/ppermute | solution.py:48
  74.1 7.7 %collective-permute-start.6 = (f32[128,512]{1,0:T(8,128)S(1)}, f32[128,512]{1,0:T(8,128)S(1)}, u32[]{:S(2)}, u32[]{:S(2)}) collective-permute-start(f32[128,512]{1,0:T(8,128)S(1)} %collective-permute-done.4), channel_id=1, source_target_pairs={{0,14},{2,0},{4,2},{6,4},{8,6},{10,8},{12,10},{14,12},{1,15},{3,1}... | collective-permute-start | bytes 786440 | tf_op jit(solution)/shard_map/ppermute | solution.py:49
  81.7 6.3 %collective-permute-start.7 = (f32[64,512]{1,0:T(8,128)S(1)}, f32[64,512]{1,0:T(8,128)S(1)}, u32[]{:S(2)}, u32[]{:S(2)}) collective-permute-start(f32[64,512]{1,0:T(8,128)S(1)} %slice.60), channel_id=1, source_target_pairs={{0,2},{2,4},{4,6},{6,8},{8,10},{10,12},{12,14},{14,0},{1,3},{3,5},... | collective-permute-start | bytes 393224 | tf_op jit(solution)/shard_map/ppermute | solution.py:52
  81.8 6.2 %collective-permute-start.8 = (f32[64,512]{1,0:T(8,128)S(1)}, f32[64,512]{1,0:T(8,128)S(1)}, u32[]{:S(2)}, u32[]{:S(2)}) collective-permute-start(f32[64,512]{1,0:T(8,128)S(1)} %slice.61), channel_id=1, source_target_pairs={{0,14},{2,0},{4,2},{6,4},{8,6},{10,8},{12,10},{14,12},{1,15},{3,1}... | collective-permute-start | bytes 393224 | tf_op jit(solution)/shard_map/ppermute | solution.py:53
  91.7 2.9 %collective-permute-start.9 = (f32[1024,256]{0,1:T(8,128)S(1)}, f32[1024,256]{0,1:T(8,128)S(1)}, u32[]{:S(2)}, u32[]{:S(2)}) collective-permute-start(f32[1024,256]{0,1:T(8,128)S(1)} %convolution_bitcast_fusion), channel_id=1, source_target_pairs={{0,16},{16,0},{1,17},{17,1},{2,18},{18,2},{3,19},{19,3},{4,20},{20... | collective-permute-start | bytes 3145736 | tf_op jit(solution)/shard_map/ppermute | solution.py:84
  99.3 20.8 %all-to-all-start.1 = ((f32[8,128,256]{1,2,0:T(8,128)}), f32[8,128,256]{1,2,0:T(8,128)S(1)}, u32[]{:S(2)}, u32[]{:S(2)}) async-start(f32[8,128,256]{1,2,0:T(8,128)} %bitcast.88), calls=%async_computation.1 | async-start | bytes 2097152 | tf_op jit(solution)/shard_map/all_to_all | solution.py:86
  105.2 112.7 %all-gather.3.cloned.1.call-start = ((), (), s32[]{:S(2)}) async-start(), calls=%async_computation.5 | async-start | bytes 2228224 | tf_op jit(solution)/shard_map/all_gather | solution.py:91
  122.2 1.4 collective-permute-start.10
  123.6 24.6 %collective-permute-start.11 = (f32[2,128,256]{1,2,0:T(8,128)S(1)}, f32[2,128,256]{1,2,0:T(8,128)S(1)}, u32[]{:S(2)}, u32[]{:S(2)}) collective-permute-start(f32[2,128,256]{1,2,0:T(8,128)S(1)} %maximum_select_fusion.1), channel_id=1, source_target_pairs={{0,0},{1,16},{2,32},{3,48},{4,64},{5,80},{6,96},{7,112},{8,128},{9... | collective-permute-start | bytes 786440 | tf_op jit(solution)/shard_map/ppermute | solution.py:96
  148.2 30.3 %collective-permute-start.12 = (f32[2,128,256]{1,2,0:T(8,128)S(1)}, f32[2,128,256]{1,2,0:T(8,128)S(1)}, u32[]{:S(2)}, u32[]{:S(2)}) collective-permute-start(f32[2,128,256]{1,2,0:T(8,128)S(1)} %collective-permute-done.11), channel_id=1, source_target_pairs={{0,2},{2,4},{4,6},{6,8},{8,10},{10,12},{12,14},{14,0},{1,3},{3,5},... | collective-permute-start | bytes 786440 | tf_op jit(solution)/shard_map/ppermute | solution.py:48
  148.2 32.2 %collective-permute-start.13 = (f32[2,128,256]{1,2,0:T(8,128)S(1)}, f32[2,128,256]{1,2,0:T(8,128)S(1)}, u32[]{:S(2)}, u32[]{:S(2)}) collective-permute-start(f32[2,128,256]{1,2,0:T(8,128)S(1)} %collective-permute-done.11), channel_id=1, source_target_pairs={{0,14},{2,0},{4,2},{6,4},{8,6},{10,8},{12,10},{14,12},{1,15},{3,1}... | collective-permute-start | bytes 786440 | tf_op jit(solution)/shard_map/ppermute | solution.py:49
  154.8 19.7 %all-to-all-start.2 = ((f32[16,16,256]{2,1,0:T(8,128)}), f32[16,16,256]{2,1,0:T(8,128)S(1)}, u32[]{:S(2)}, u32[]{:S(2)}) async-start(f32[16,16,256]{2,1,0:T(8,128)} %fusion.11), calls=%async_computation.2 | async-start | bytes 524288 | tf_op jit(solution)/shard_map/all_to_all | solution.py:102
  175.2 13.4 %all-to-all-start.3 = ((f32[8,16,256]{2,1,0:T(8,128)}), f32[8,16,256]{2,1,0:T(8,128)S(1)}, u32[]{:S(2)}, u32[]{:S(2)}) async-start(f32[8,16,256]{2,1,0:T(8,128)} %broadcast_in_dim.89), calls=%async_computation.3 | async-start | bytes 262144 | tf_op jit(solution)/shard_map/all_to_all | solution.py:104
  178.5 15.6 %collective-permute-start.14 = (f32[2,128,256]{1,2,0:T(8,128)S(1)}, f32[2,128,256]{1,2,0:T(8,128)}, u32[]{:S(2)}, u32[]{:S(2)}) collective-permute-start(f32[2,128,256]{1,2,0:T(8,128)S(1)} %collective-permute-done.12), channel_id=1, source_target_pairs={{0,2},{2,4},{4,6},{6,8},{8,10},{10,12},{12,14},{14,0},{1,3},{3,5},... | collective-permute-start | bytes 786440 | tf_op jit(solution)/shard_map/ppermute | solution.py:48
  180.5 14.4 %collective-permute-start.15 = (f32[2,128,256]{1,2,0:T(8,128)S(1)}, f32[2,128,256]{1,2,0:T(8,128)}, u32[]{:S(2)}, u32[]{:S(2)}) collective-permute-start(f32[2,128,256]{1,2,0:T(8,128)S(1)} %collective-permute-done.13), channel_id=1, source_target_pairs={{0,14},{2,0},{4,2},{6,4},{8,6},{10,8},{12,10},{14,12},{1,15},{3,1}... | collective-permute-start | bytes 786440 | tf_op jit(solution)/shard_map/ppermute | solution.py:49
  189.4 27.6 %all-to-all-start.4 = ((f32[32,16,256]{2,1,0:T(8,128)}), f32[32,16,256]{2,1,0:T(8,128)S(1)}, u32[]{:S(2)}, u32[]{:S(2)}) async-start(f32[32,16,256]{2,1,0:T(8,128)} %broadcast_in_dim.90), calls=%async_computation.4 | async-start | bytes 1048576 | tf_op jit(solution)/shard_map/all_to_all | solution.py:106
  194.2 9.9 %collective-permute-start.16 = (f32[2,128,256]{1,2,0:T(8,128)}, f32[2,128,256]{1,2,0:T(8,128)S(1)}, u32[]{:S(2)}, u32[]{:S(2)}) collective-permute-start(f32[2,128,256]{1,2,0:T(8,128)} %collective-permute-done.14), channel_id=1, source_target_pairs={{0,2},{2,4},{4,6},{6,8},{8,10},{10,12},{12,14},{14,0},{1,3},{3,5},... | collective-permute-start | bytes 786440 | tf_op jit(solution)/shard_map/ppermute | solution.py:48
  194.8 9.2 %collective-permute-start.17 = (f32[2,128,256]{1,2,0:T(8,128)}, f32[2,128,256]{1,2,0:T(8,128)S(1)}, u32[]{:S(2)}, u32[]{:S(2)}) collective-permute-start(f32[2,128,256]{1,2,0:T(8,128)} %collective-permute-done.15), channel_id=1, source_target_pairs={{0,14},{2,0},{4,2},{6,4},{8,6},{10,8},{12,10},{14,12},{1,15},{3,1}... | collective-permute-start | bytes 786440 | tf_op jit(solution)/shard_map/ppermute | solution.py:49
  204.0 8.7 %collective-permute-start.18 = (f32[2,64,256]{1,2,0:T(8,128)S(1)}, f32[2,64,256]{1,2,0:T(8,128)S(1)}, u32[]{:S(2)}, u32[]{:S(2)}) collective-permute-start(f32[2,64,256]{1,2,0:T(8,128)S(1)} %bitcast.103), channel_id=1, source_target_pairs={{0,2},{2,4},{4,6},{6,8},{8,10},{10,12},{12,14},{14,0},{1,3},{3,5},... | collective-permute-start | bytes 393224 | tf_op jit(solution)/shard_map/ppermute | solution.py:52
  204.9 10.4 %collective-permute-start.19 = (f32[2,64,256]{1,2,0:T(8,128)}, f32[2,64,256]{1,2,0:T(8,128)}, u32[]{:S(2)}, u32[]{:S(2)}) collective-permute-start(f32[2,64,256]{1,2,0:T(8,128)} %slice.65), channel_id=1, source_target_pairs={{0,14},{2,0},{4,2},{6,4},{8,6},{10,8},{12,10},{14,12},{1,15},{3,1}... | collective-permute-start | bytes 393224 | tf_op jit(solution)/shard_map/ppermute | solution.py:53
  213.4 3.6 %copy-start.1 = (f32[2,256,256]{2,1,0:T(8,128)S(1)}, f32[2,256,256]{2,1,0:T(8,128)}, u32[]{:S(2)}) copy-start(f32[2,256,256]{2,1,0:T(8,128)} %param.7) | copy-start | bytes 1572868
Sparse Core Ops, SparseCore 0:
  121.6 48.0 all-gather.2
